TPU v7x, 512 devices: a whole 4x4x16 slice. The times are simulated.
512 devices in a mesh: layer: 8 (over x, core), prow: 4 (over y), pcol: 16 (over z).
Axes of the slice: x: 4, y: 4, z: 16, core: 2. Of those that a mesh axis runs over, the one named last changes fastest.
Arguments:
- rhs: bfloat16 [8, 3, 16, 64, 128], P('layer', None, 'prow'), may hold values from -6 to 6
- diag_low: bfloat16 [8, 3, 16, 128, 128], P('layer', None, 'prow'), may hold values from -1 to 2
- diag_up: bfloat16 [8, 3, 16, 128, 128], P('layer', None, 'pcol'), may hold values from -1 to 2
- low_blocks: bfloat16 [8, 2, 16, 16, 128, 128], P('layer', None, 'prow', 'pcol'), may hold values from -0.1875 to 0.1875
- up_blocks: bfloat16 [8, 2, 16, 16, 128, 128], P('layer', None, 'prow', 'pcol'), may hold values from -0.1875 to 0.1875
- pattern: int32 [8, 2, 16, 16], P('layer', None, 'prow', 'pcol'), may hold values 0 or 1
- sub_sizes: int32 [8, 3, 16], P('layer'), may hold values from 32 to 128
- anc_rhs: bfloat16 [16, 64, 128], P('prow'), may hold values from -6 to 6
- anc_dl: bfloat16 [16, 128, 128], P('prow'), may hold values from -1 to 2
- anc_du: bfloat16 [16, 128, 128], P('prow'), may hold values from -1 to 2
- anc_low: bfloat16 [8, 16, 16, 128, 128], P('layer', 'prow', 'pcol'), may hold values from -0.0625 to 0.0625
- anc_up: bfloat16 [8, 16, 16, 128, 128], P('layer', 'prow', 'pcol'), may hold values from -0.1875 to 0.1875
- anc_pattern: int32 [8, 16, 16], P('layer', 'prow', 'pcol'), may hold values 0 or 1
Outputs:
- solution: bfloat16 [8, 3, 16, 64, 128], P('layer', None, 'pcol')
- anc_solution: bfloat16 [16, 64, 128], P('prow')
All inputs are finite; a program needn't handle non-finite values. No bound on the sum of `pattern` or of `anc_pattern` on one device may be relied on, other than what follows from the above.
Results may differ from a plain program's by a relative error of at most 0.019.
Values may be sent and summed in bfloat16 or wider, within the bound.
A program may use at most 64 MiB of HBM per device.

v0:
```python
import jax
import jax.numpy as jnp
from jax import lax
from jax.sharding import PartitionSpec as P


def broadcast(value, axis, source):
    kept = jnp.where(lax.axis_index(axis) == source, value, 0).astype(value.dtype)
    return lax.psum(kept, axis)


def apply_inverse(known, partial_value, inverse, live_mask):
    lowered = (known.astype(jnp.float32) - partial_value).astype(jnp.bfloat16)
    solved = jnp.einsum("irs,ist->irt", lowered, inverse, preferred_element_type=jnp.float32)
    return jnp.where(live_mask, solved, 0.0).astype(jnp.bfloat16)


def child_sums(segments, blocks, links):
    products = jnp.einsum("jrs,ijst->ijrt", segments, blocks, preferred_element_type=jnp.float32)
    return jnp.sum(products * links.astype(jnp.float32)[:, :, None, None], axis=1)


def parent_sums(segments, blocks, links):
    products = jnp.einsum("irs,ijst->ijrt", segments, blocks, preferred_element_type=jnp.float32)
    return jnp.sum(products * links.astype(jnp.float32)[:, :, None, None], axis=0)


def live_columns(sizes_row, columns_count):
    positions = lax.iota(jnp.int32, columns_count)
    return positions[None, None, :] < sizes_row[:, None, None]


def per_device(
    rhs,
    diag_low,
    diag_up,
    low_blocks,
    up_blocks,
    pattern,
    sub_sizes,
    anc_rhs,
    anc_dl,
    anc_du,
    anc_low,
    anc_up,
    anc_pattern,
):
    grid_row = lax.axis_index("prow")
    grid_col = lax.axis_index("pcol")
    col_group = lax.axis_size("pcol") // lax.axis_size("prow")
    levels = rhs.shape[1]
    columns_count = rhs.shape[-1]
    row_count = rhs.shape[2]
    col_count = diag_up.shape[2]
    sizes_all = sub_sizes[0]
    segments_kept = []
    carried = None
    for level_index in range(levels):
        known = rhs[0, level_index]
        inverse = diag_low[0, level_index]
        row_sizes = lax.dynamic_slice_in_dim(
            sizes_all[level_index], grid_row * row_count, row_count
        )
        live_mask = live_columns(row_sizes, columns_count)
        if level_index == 0:
            block_rows = apply_inverse(
                known, jnp.zeros(known.shape, jnp.float32), inverse, live_mask
            )
        else:
            partial_value = child_sums(
                carried, low_blocks[0, level_index - 1], pattern[0, level_index - 1]
            )
            summed = lax.psum(partial_value, "pcol")
            block_rows = apply_inverse(known, summed, inverse, live_mask)
        own_cols = lax.dynamic_slice_in_dim(
            block_rows, grid_col % col_group * col_count, col_count, 0
        )
        carried = broadcast(own_cols, "prow", grid_col // col_group)
        segments_kept.append(carried)
    anc_partial = child_sums(carried, anc_low[0], anc_pattern[0])
    anc_total = lax.psum(anc_partial, ("layer", "pcol"))
    anc_forward = apply_inverse(anc_rhs, anc_total, anc_dl, True)
    anc_solution = jnp.einsum(
        "irs,ist->irt", anc_forward, anc_du, preferred_element_type=jnp.float32
    ).astype(jnp.bfloat16)
    columns = [None] * levels
    parent_rows = anc_solution
    for level_index in reversed(range(levels)):
        if level_index == levels - 1:
            partial_value = parent_sums(parent_rows, anc_up[0], anc_pattern[0])
        else:
            partial_value = parent_sums(
                parent_rows, up_blocks[0, level_index], pattern[0, level_index]
            )
        inverse = diag_up[0, level_index]
        col_sizes = lax.dynamic_slice_in_dim(
            sizes_all[level_index], grid_col * col_count, col_count
        )
        live_mask = live_columns(col_sizes, columns_count)
        known = segments_kept[level_index]
        summed = lax.psum(partial_value, "prow")
        column_rows = apply_inverse(known, summed, inverse, live_mask)
        columns[level_index] = column_rows
        if level_index > 0:
            whole_level = lax.all_gather(column_rows, "pcol", axis=0, tiled=True)
            parent_rows = lax.dynamic_slice_in_dim(whole_level, grid_row * row_count, row_count, 0)
    return (jnp.stack(columns)[None], anc_solution)


def solution(mesh):
    return jax.shard_map(
        per_device,
        mesh=mesh,
        in_specs=(
            P("layer", None, "prow", None, None),
            P("layer", None, "prow", None, None),
            P("layer", None, "pcol", None, None),
            P("layer", None, "prow", "pcol", None, None),
            P("layer", None, "prow", "pcol", None, None),
            P("layer", None, "prow", "pcol"),
            P("layer", None, None),
            P("prow", None, None),
            P("prow", None, None),
            P("prow", None, None),
            P("layer", "prow", "pcol", None, None),
            P("layer", "prow", "pcol", None, None),
            P("layer", "prow", "pcol"),
        ),
        out_specs=(P("layer", None, "pcol", None, None), P("prow", None, None)),
        check_vma=False,
    )
```

profile of v0, /device:TPU:6, one launch (start us, length us, event | category | flops | bytes accessed | tf_op | source)
XLA Modules:
  0.0 759.7 jit_solution(10889565686120879335)
XLA Ops:
  7.2 0.0 copy-start
  7.2 0.0 all-reduce.4.cloned.1.call-start
  7.3 0.7 convert_bitcast_fusion.2
  8.0 0.7 fusion.65
  8.7 0.1 fusion.62
  8.7 0.1 iota_compare_fusion.2
  8.8 1.1 fusion.24
  10.0 0.0 copy-start.11
  10.0 17.2 %psum.63 = bf16[1,64,128]{2,1,0:T(8,128)(2,1)S(1)} all-reduce(bf16[1,64,128]{2,1,0:T(8,128)(2,1)S(1)} %fusion.54), channel_id=1, replica_groups=mesh['layer'=8,'prow'=4,'pcol'=16] {'prow'}, use_global_device_ids=true, to_apply=%region_0.1 | all-reduce | flops 8192 | bytes 32768 | tf_op jit(solution)/shard_map/psum | solution.py:9
  27.1 0.8 fusion.8
  27.9 0.0 all-reduce.4.cloned.1.call-update
  28.0 0.0 all-reduce.6.cloned.1.call-start
  28.0 0.6 constant_dynamic-slice_fusion.8
  28.6 0.1 fusion.64
  28.7 0.1 iota_compare_fusion
  28.8 0.1 iota_compare_fusion.1
  28.9 0.6 iota_compare_fusion.5
  29.5 135.1 %all-reduce.4.cloned.1.call-done = f32[4,64,128]{2,1,0:T(8,128)} async-done(((f32[4,64,128]{2,1,0:T(8,128)}), f32[4,64,128]{2,1,0:T(8,128)}) %all-reduce.4.cloned.1.call-update) | async-done | bytes 131088 | tf_op jit(solution)/shard_map/psum | solution.py:73
  164.7 1.1 fusion.22
  165.8 16.9 %psum.65 = bf16[1,64,128]{2,1,0:T(8,128)(2,1)S(1)} all-reduce(bf16[1,64,128]{2,1,0:T(8,128)(2,1)S(1)} %fusion.55), channel_id=1, replica_groups=mesh['layer'=8,'prow'=4,'pcol'=16] {'prow'}, use_global_device_ids=true, to_apply=%region_2.3 | all-reduce | flops 8192 | bytes 32768 | tf_op jit(solution)/shard_map/psum | solution.py:9
  182.6 0.8 fusion.6
  183.5 0.0 all-reduce.6.cloned.1.call-update
  183.5 0.0 all-reduce.8.cloned.1.call-start
  183.5 0.6 constant_dynamic-slice_fusion.4
  184.1 0.6 iota_compare_fusion.3
  184.8 128.0 %all-reduce.6.cloned.1.call-done = f32[4,64,128]{2,1,0:T(8,128)} async-done(((f32[4,64,128]{2,1,0:T(8,128)}), f32[4,64,128]{2,1,0:T(8,128)}) %all-reduce.6.cloned.1.call-update) | async-done | bytes 131088 | tf_op jit(solution)/shard_map/psum | solution.py:73
  312.8 1.1 fusion.20
  313.8 16.9 %psum.67 = bf16[1,64,128]{2,1,0:T(8,128)(2,1)S(1)} all-reduce(bf16[1,64,128]{2,1,0:T(8,128)(2,1)S(1)} %fusion.56), channel_id=1, replica_groups=mesh['layer'=8,'prow'=4,'pcol'=16] {'prow'}, use_global_device_ids=true, to_apply=%region_4.5 | all-reduce | flops 8192 | bytes 32768 | tf_op jit(solution)/shard_map/psum | solution.py:9
  330.8 0.8 fusion.4
  331.6 0.0 all-reduce.8.cloned.1.call-update
  331.6 0.7 iota_compare_fusion.4
  332.3 313.2 %all-reduce.8.cloned.1.call-done = f32[4,64,128]{2,1,0:T(8,128)} async-done(((f32[4,64,128]{2,1,0:T(8,128)}), f32[4,64,128]{2,1,0:T(8,128)}) %all-reduce.8.cloned.1.call-update) | async-done | bytes 131088 | tf_op jit(solution)/shard_map/psum | solution.py:81
  645.5 1.2 convolution_convert_fusion
  646.7 0.0 copy-done.5
  646.7 0.0 copy-start.3
  646.7 0.2 fusion.9
  646.9 0.4 copy-done.3
  647.3 17.2 %psum.69 = f32[1,64,128]{2,1,0:T(8,128)S(1)} all-reduce(f32[1,64,128]{2,1,0:T(8,128)S(1)} %bitcast.179), channel_id=1, replica_groups=mesh['layer'=8,'prow'=4,'pcol'=16] {'prow'}, use_global_device_ids=true, to_apply=%region_7.8 | all-reduce | flops 8192 | bytes 65536 | tf_op jit(solution)/shard_map/psum | solution.py:101
  664.5 0.1 fusion.12
  664.6 27.4 %all-gather = bf16[1024,128]{1,0:T(8,128)(2,1)S(1)} all-gather(bf16[64,128]{1,0:T(8,128)(2,1)S(1)} %fusion.12), channel_id=2, replica_groups=mesh['layer'=8,'prow'=4,'pcol'=16] {'pcol'}, dimensions={0}, use_global_device_ids=true | all-gather | bytes 278528 | tf_op jit(solution)/shard_map/all_gather | solution.py:105
  692.1 0.2 fusion.10
  692.2 14.4 %psum.70 = f32[1,64,128]{2,1,0:T(8,128)S(1)} all-reduce(f32[1,64,128]{2,1,0:T(8,128)S(1)} %bitcast.181), channel_id=1, replica_groups=mesh['layer'=8,'prow'=4,'pcol'=16] {'prow'}, use_global_device_ids=true, to_apply=%region_9.10 | all-reduce | flops 8192 | bytes 65536 | tf_op jit(solution)/shard_map/psum | solution.py:101
  706.7 0.1 fusion.13
  706.8 29.2 %all-gather.1 = bf16[1024,128]{1,0:T(8,128)(2,1)S(1)} all-gather(bf16[64,128]{1,0:T(8,128)(2,1)S(1)} %fusion.13), channel_id=3, replica_groups=mesh['layer'=8,'prow'=4,'pcol'=16] {'pcol'}, dimensions={0}, use_global_device_ids=true | all-gather | bytes 278528 | tf_op jit(solution)/shard_map/all_gather | solution.py:105
  736.0 0.2 fusion.11
  736.2 16.2 %psum.71 = f32[1,64,128]{2,1,0:T(8,128)S(1)} all-reduce(f32[1,64,128]{2,1,0:T(8,128)S(1)} %bitcast.180), channel_id=1, replica_groups=mesh['layer'=8,'prow'=4,'pcol'=16] {'prow'}, use_global_device_ids=true, to_apply=%region_11.12 | all-reduce | flops 8192 | bytes 65536 | tf_op jit(solution)/shard_map/psum | solution.py:101
  752.4 0.1 fusion.15
  752.6 0.6 maximum_bitcast_fusion
  (26 shorter events, 0.1 us)
Async XLA Ops:
  7.2 323.6 %copy-start = (bf16[1,4,1,128,128]{4,3,2,1,0:T(8,128)(2,1)S(1)}, bf16[1,4,1,128,128]{4,3,2,1,0:T(8,128)(2,1)}, u32[]{:S(2)}) copy-start(bf16[1,4,1,128,128]{4,3,2,1,0:T(8,128)(2,1)} %param.23) | copy-start | bytes 393220
  7.2 20.0 %copy-start.2 = (bf16[1,2,4,1,128,128]{5,4,3,2,1,0:T(8,128)(2,1)S(1)}, bf16[1,2,4,1,128,128]{5,4,3,2,1,0:T(8,128)(2,1)}, u32[]{:S(2)}) copy-start(bf16[1,2,4,1,128,128]{5,4,3,2,1,0:T(8,128)(2,1)} %param.16) | copy-start | bytes 786436
  7.2 157.5 %all-reduce.4.cloned.1.call-start = ((), (), s32[]{:S(2)}) async-start(), calls=%async_computation | async-start | bytes 262144 | tf_op jit(solution)/shard_map/psum | solution.py:73
  8.7 156.0 %copy-start.1 = (bf16[1,3,4,128,128]{4,3,2,1,0:T(8,128)(2,1)S(1)}, bf16[1,3,4,128,128]{4,3,2,1,0:T(8,128)(2,1)}, u32[]{:S(2)}) copy-start(bf16[1,3,4,128,128]{4,3,2,1,0:T(8,128)(2,1)} %param.14) | copy-start | bytes 1179652
  10.0 18.1 %copy-start.11 = (s32[1,4,1]{1,2,0:T(1,128)S(1)}, s32[1,4,1]{1,2,0:T(1,128)}, u32[]{:S(2)}) copy-start(s32[1,4,1]{1,2,0:T(1,128)} %param.25) | copy-start | bytes 52
  27.1 137.5 %copy-start.4 = (bf16[1,3,4,64,128]{4,3,2,1,0:T(8,128)(2,1)S(1)}, bf16[1,3,4,64,128]{4,3,2,1,0:T(8,128)(2,1)}, u32[]{:S(2)}) copy-start(bf16[1,3,4,64,128]{4,3,2,1,0:T(8,128)(2,1)} %param.13) | copy-start | bytes 589828
  28.0 284.8 %all-reduce.6.cloned.1.call-start = ((), (), s32[]{:S(2)}) async-start(), calls=%async_computation.1 | async-start | bytes 262144 | tf_op jit(solution)/shard_map/psum | solution.py:73
  183.5 462.0 %all-reduce.8.cloned.1.call-start = ((), (), s32[]{:S(2)}) async-start(), calls=%async_computation.2 | async-start | bytes 262144 | tf_op jit(solution)/shard_map/psum | solution.py:81
  330.7 314.7 %copy-start.7 = (bf16[4,128,128]{2,1,0:T(8,128)(2,1)S(1)}, bf16[4,128,128]{2,1,0:T(8,128)(2,1)}, u32[]{:S(2)}) copy-start(bf16[4,128,128]{2,1,0:T(8,128)(2,1)} %param.21) | copy-start | bytes 393220
  330.7 314.7 %copy-start.9 = (bf16[4,64,128]{2,1,0:T(8,128)(2,1)S(1)}, bf16[4,64,128]{2,1,0:T(8,128)(2,1)}, u32[]{:S(2)}) copy-start(bf16[4,64,128]{2,1,0:T(8,128)(2,1)} %param.20) | copy-start | bytes 196612
  331.6 313.9 %copy-start.6 = (bf16[4,128,128]{2,1,0:T(8,128)(2,1)S(1)}, bf16[4,128,128]{2,1,0:T(8,128)(2,1)}, u32[]{:S(2)}) copy-start(bf16[4,128,128]{2,1,0:T(8,128)(2,1)} %param.22) | copy-start | bytes 393220
  332.3 314.4 %copy-start.5 = (bf16[1,4,1,128,128]{4,3,2,1,0:T(8,128)(2,1)S(1)}, bf16[1,4,1,128,128]{4,3,2,1,0:T(8,128)(2,1)}, u32[]{:S(2)}) copy-start(bf16[1,4,1,128,128]{4,3,2,1,0:T(8,128)(2,1)} %param.24) | copy-start | bytes 393220
  646.7 0.6 copy-start.3
  646.7 17.8 %copy-start.8 = (bf16[1,3,1,128,128]{4,3,2,1,0:T(8,128)(2,1)S(1)}, bf16[1,3,1,128,128]{4,3,2,1,0:T(8,128)(2,1)}, u32[]{:S(2)}) copy-start(bf16[1,3,1,128,128]{4,3,2,1,0:T(8,128)(2,1)} %param.15) | copy-start | bytes 294916
  647.3 44.7 %copy-start.10 = (bf16[1,2,4,1,128,128]{5,4,3,2,1,0:T(8,128)(2,1)S(1)}, bf16[1,2,4,1,128,128]{5,4,3,2,1,0:T(8,128)(2,1)}, u32[]{:S(2)}) copy-start(bf16[1,2,4,1,128,128]{5,4,3,2,1,0:T(8,128)(2,1)} %param.17) | copy-start | bytes 786436
Sparse Core Ops, SparseCore 0:
  28.1 136.5 all-reduce.3
  183.6 129.1 all-reduce.5
  331.7 313.7 all-reduce.7
where the time goes:
time: 761 us; the launch traced here: 760 us
  waiting for transfers between devices  576 us (76%)
  blocking collectives  155 us (20%)
  between operations  14 us (2%)
  matrix products  7.68 us (1%)
    psum x1, waiting for transfers between devices, per_device(): anc_total = lax.psum(anc_partial, ('layer', 'pcol'))  313 us
    psum x2, waiting for transfers between devices, per_device(): summed = lax.psum(partial_value, 'pcol')  263 us
    all_gather x2, blocking collectives, per_device(): whole_level = lax.all_gather(column_rows, 'pcol', axis=0, tiled=True)  56.7 us
    psum x3, blocking collectives, broadcast(): return lax.psum(kept, axis)  50.9 us
    psum x3, blocking collectives, per_device(): summed = lax.psum(partial_value, 'prow')  47.8 us
  transfers between devices with their start and end apart: 3, of which 3 were waited for; matrix products, arithmetic and copies ran while one was open for 0% of the time, Pallas kernels for 0%

commit v1 on v0

v1 whole, which is shorter than its diff:
```python
import functools

import jax
import jax.numpy as jnp
from jax import lax
from jax.experimental import pallas as pl
from jax.experimental.pallas import tpu as pltpu
from jax.sharding import PartitionSpec as P

MESH = pl.DeviceIdType.MESH
BF16 = jnp.bfloat16
F32 = jnp.float32


def far_first(n):
    return sorted(range(1, n), key=lambda d: (-min(d, n - d), d))


def dot(a, b):
    return jnp.dot(a, b, preferred_element_type=F32)


def kernel(
    nl, ny, nz, levels, rows, rq, S,
    rhs, diag_low, diag_up, low, up, pattern, sizes,
    anc_rhs, anc_dl, anc_du, anc_low, anc_up, anc_pattern,
    osol, oanc,
    pat_v, apat_v, size_v, raw, dmine, rfull, f0, dup, quarter,
    fset, bset,
    fsrc, frecv, lrecv, ag, final,
    in_sem, own_sem, far_sem, set_send, set_recv, one_send, one_recv,
    fs_sem, fr_sem, l_send, l_recv, ag_send, ag_recv, oa_send, oa_recv, os_send, os_recv,
):
    k = lax.axis_index("layer")
    p = lax.axis_index("prow")
    c = lax.axis_index("pcol")
    j = lax.rem(c, rows)
    owner = p == c // rows
    nset = 2 * levels
    y_order, z_order, l_order = far_first(ny), far_first(nz), far_first(nl)

    def y_peer(d):
        return (k, lax.rem(p + d, ny), c)

    def z_peer(d):
        return (k, p, lax.rem(c + d, nz))

    def l_peer(d):
        return (lax.rem(k + d, nl), p, c)

    def drain(ref, sem):
        pltpu.make_async_copy(ref, ref, sem).wait()

    def remote(src, dst, send, recv, device):
        return pltpu.make_async_remote_copy(
            src_ref=src, dst_ref=dst, send_sem=send, recv_sem=recv,
            device_id=device, device_id_type=MESH,
        )

    reach = nz // 4
    near = [d for d in z_order if min(d, nz - d) <= reach]
    barrier = pltpu.get_barrier_semaphore()
    greeted = [z_peer(d) for d in near] + [y_peer(d) for d in y_order] + [l_peer(d) for d in l_order]
    for device in greeted:
        pl.semaphore_signal(barrier, inc=1, device_id=device, device_id_type=MESH)

    def fetch(src, dst, n):
        copy = pltpu.make_async_copy(src, dst, in_sem.at[n])
        copy.start()
        return copy

    sets_in = [low.at[0, l, :, 0] for l in range(levels - 1)] + [anc_low.at[0, :, 0], anc_up.at[0, :, 0]]
    sets_in += [up.at[0, l, :, 0] for l in reversed(range(levels - 1))]
    got_pat = fetch(pattern, pat_v, 0)
    got_apat = fetch(anc_pattern, apat_v, 1)
    got_size = fetch(sizes, size_v, 2)
    got_sets = [fetch(sets_in[0], raw.at[0], 3)]
    own = [
        pltpu.make_async_copy(diag_low.at[0, :, j], dmine.at[pl.ds(0, levels)], own_sem.at[0]),
        pltpu.make_async_copy(rhs.at[0, :, j], rfull.at[pl.ds(0, levels)], own_sem.at[1]),
        pltpu.make_async_copy(anc_rhs.at[j], rfull.at[levels], own_sem.at[2]),
        pltpu.make_async_copy(anc_dl.at[j], dmine.at[levels], own_sem.at[3]),
        pltpu.make_async_copy(anc_du.at[j], dmine.at[levels + 1], own_sem.at[4]),
    ]

    @pl.when(owner)
    def _():
        for copy in own:
            copy.start()

    for n in range(1, nset):
        got_sets.append(fetch(sets_in[n], raw.at[n], 3 + n))
    got_dup = fetch(diag_up.at[0, :, 0], dup, 3 + nset)

    def link(n, i):
        if n < levels - 1:
            return pat_v[0, n, i, 0]
        if n < levels + 1:
            return apat_v[0, i, 0]
        return pat_v[0, nset - 1 - n, i, 0]

    def mask_set(n):
        got_sets[n].wait()
        for i in range(rows):
            present = jnp.full((S, S), link(n, i), jnp.int32).astype(F32).astype(BF16)
            block = raw[n, i] * present
            if n < levels:
                fset[n, p, :, i * S:(i + 1) * S] = block
            else:
                bset[n - levels, p, i * S:(i + 1) * S, :] = block

    set_copies = []

    def send_set(n):
        part = fset.at[n, p] if n < levels else bset.at[n - levels, p]
        for m, d in enumerate(y_order):
            copy = remote(part, part, set_send.at[n, m], set_recv.at[n], y_peer(d))
            copy.start()
            set_copies.append(copy)

    def wait_set(n):
        whole = fset.at[n] if n < levels else bset.at[n - levels]
        drain(whole.at[pl.ds(0, ny - 1)], set_recv.at[n])

    def live(level, value):
        columns = lax.broadcasted_iota(jnp.int32, value.shape, 1)
        return jnp.where(columns < size_v[0, level, c], value, 0.0).astype(BF16)

    got_pat.wait()
    got_apat.wait()
    got_size.wait()
    mask_set(0)

    @pl.when(owner)
    def _():
        for copy in own[:3]:
            copy.wait()
        f0[...] = live(0, dot(rfull[0], dmine[0]))
        mine = pl.ds(pl.multiple_of(p * rq, rq), rq)
        quarter[0] = f0[mine]
        for n in range(levels):
            quarter[n + 1] = rfull[n + 1, mine]

    pl.semaphore_wait(barrier, len(greeted))
    for d in (reach, nz - reach):
        pl.semaphore_signal(far_sem, inc=1, device_id=z_peer(d), device_id_type=MESH)

    def one_copies(m, d):
        theirs = pl.ds(pl.multiple_of(lax.rem(p + d, ny) * rq, rq), rq)
        pairs = [
            (f0.at[theirs], quarter.at[0]),
            (rfull.at[pl.ds(1, levels), theirs], quarter.at[pl.ds(1, levels)]),
            (dmine.at[1], dmine.at[1]),
            (dmine.at[pl.ds(2, levels)], dmine.at[pl.ds(2, levels)]),
        ]
        return [
            remote(src, dst, one_send.at[n, m], one_recv.at[n], y_peer(d))
            for n, (src, dst) in enumerate(pairs)
        ]

    one_all = [one_copies(m, d) for m, d in enumerate(y_order)]

    def send_one(n):
        @pl.when(owner)
        def _():
            for copies in one_all:
                copies[n].start()

    def wait_one(n):
        @pl.when(jnp.logical_not(owner))
        def _():
            one_all[0][n].wait_recv()

    send_one(0)
    send_set(0)
    send_one(1)
    send_one(2)
    mask_set(1)
    send_set(1)

    @pl.when(owner)
    def _():
        for copy in own[3:]:
            copy.wait()

    send_one(3)
    for n in range(2, nset):
        mask_set(n)
        send_set(n)

    segment = None
    forward = []
    for level in range(levels + 1):
        if level == 0:
            wait_one(0)
            segment = quarter[0]
            forward.append(segment)
            continue
        n = level - 1
        wait_set(n)
        for s in range(ny):
            product = dot(segment, fset[n, s])
            for i in range(rows):
                fsrc[n, s * rows + i] = product[:, i * S:(i + 1) * S].astype(BF16)
        if n == 0:
            pl.semaphore_wait(far_sem, 2)
        for d in z_order:
            target = lax.rem(c + d, nz)
            remote(fsrc.at[n, target], frecv.at[n, d - 1], fs_sem.at[n], fr_sem.at[n], z_peer(d)).start()
        if level == 1:
            wait_one(1)
            wait_one(2)
        if level == 2:
            wait_one(3)
        drain(frecv.at[n], fr_sem.at[n])
        total = fsrc[n, c].astype(F32)
        for d in range(1, nz):
            total = total + frecv[n, d - 1].astype(F32)
        if level < levels:
            lowered = (quarter[level].astype(F32) - total).astype(BF16)
            segment = live(level, dot(lowered, dmine[level]))
            forward.append(segment)

    lrecv[k] = total.astype(BF16)
    for d in l_order:
        remote(lrecv.at[k], lrecv.at[k], l_send, l_recv, l_peer(d)).start()
    drain(lrecv.at[pl.ds(0, nl - 1)], l_recv)
    total = lrecv[0].astype(F32)
    for n in range(1, nl):
        total = total + lrecv[n].astype(F32)
    lowered = (quarter[levels].astype(F32) - total).astype(BF16)
    afwd = dot(lowered, dmine[levels]).astype(BF16)
    solved = dot(afwd, dmine[levels + 1]).astype(BF16)

    mine = pl.ds(pl.multiple_of(p * rq, rq), rq)
    got_dup.wait()
    sol_copies = []
    anc_copies = []
    for step in range(levels + 1):
        level = levels - step
        if level < levels:
            osol[0, level, 0, mine] = solved
            part = osol.at[0, level, 0, mine]
            for m, d in enumerate(y_order):
                copy = remote(part, part, os_send.at[level, m], os_recv.at[level], y_peer(d))
                copy.start()
                sol_copies.append(copy)
        if level == 0:
            break
        ag[step, c] = solved
        for d in z_order:
            remote(ag.at[step, c], ag.at[step, c], ag_send.at[step], ag_recv.at[step], z_peer(d)).start()
        wait_set(levels + step)
        drain(ag.at[step, pl.ds(0, nz - 1)], ag_recv.at[step])
        if step == 0:
            for i in range(rows):
                oanc[i, mine] = ag[0, p * rows + i]
                for m, d in enumerate(y_order):
                    theirs = lax.rem(p + d, ny) * rows + i
                    copy = remote(ag.at[0, theirs], oanc.at[i, mine], oa_send.at[i, m], oa_recv, y_peer(d))
                    copy.start()
                    anc_copies.append(copy)
        total = None
        for s in range(ny):
            parents = jnp.concatenate([ag[step, s * rows + i] for i in range(rows)], axis=1)
            product = dot(parents, bset[step, s])
            total = product if total is None else total + product
        below = level - 1
        lowered = (forward[below].astype(F32) - total).astype(BF16)
        solved = live(below, dot(lowered, dup[below]))

    for level in reversed(range(levels)):
        drain(osol.at[0, level, 0, pl.ds(0, (ny - 1) * rq)], os_recv.at[level])
    drain(oanc.at[:, pl.ds(0, (ny - 1) * rq)], oa_recv)
    for copy in set_copies + sol_copies + anc_copies:
        copy.wait_send()

    @pl.when(owner)
    def _():
        for copies in one_all:
            for copy in copies:
                copy.wait_send()

    for n in range(levels):
        drain(frecv.at[n], fs_sem.at[n])
        drain(ag.at[n, pl.ds(0, nz - 1)], ag_send.at[n])
    drain(lrecv.at[pl.ds(0, nl - 1)], l_send)


def per_device(nl, ny, nz, *operands):
    rhs, diag_low = operands[0], operands[1]
    anc_rhs = operands[7]
    levels, rows, R, S = rhs.shape[1:]
    rq = R // ny
    nset = 2 * levels
    dma = pltpu.SemaphoreType.DMA
    scratch = [
        pltpu.SMEM(operands[5].shape, jnp.int32),
        pltpu.SMEM(operands[12].shape, jnp.int32),
        pltpu.SMEM(operands[6].shape, jnp.int32),
        pltpu.VMEM((nset, rows, S, S), BF16),
        pltpu.VMEM((levels + 2, S, S), BF16),
        pltpu.VMEM((levels + 1, R, S), BF16),
        pltpu.VMEM((R, S), BF16),
        pltpu.VMEM((levels, S, S), BF16),
        pltpu.VMEM((levels + 1, rq, S), BF16),
        pltpu.VMEM((levels, ny, S, rows * S), BF16),
        pltpu.VMEM((levels, ny, rows * S, S), BF16),
        pltpu.VMEM((levels, nz, rq, S), BF16),
        pltpu.VMEM((levels, nz - 1, rq, S), BF16),
        pltpu.VMEM((nl, rq, S), BF16),
        pltpu.VMEM((levels, nz, rq, S), BF16),
        pltpu.VMEM((rq, S), BF16),
        dma((4 + nset,)), dma((5,)), pltpu.SemaphoreType.REGULAR,
        dma((nset, ny - 1)), dma((nset,)), dma((4, ny - 1)), dma((4,)),
        dma((levels,)), dma((levels,)), dma, dma, dma((levels,)), dma((levels,)),
        dma((rows, ny - 1)), dma, dma((levels, ny - 1)), dma((levels,)),
    ]
    return pl.pallas_call(
        functools.partial(kernel, nl, ny, nz, levels, rows, rq, S),
        out_shape=(
            jax.ShapeDtypeStruct((1, levels, 1, R, S), BF16),
            jax.ShapeDtypeStruct((rows, R, S), BF16),
        ),
        in_specs=[pl.BlockSpec(memory_space=pl.ANY)] * len(operands),
        out_specs=(pl.BlockSpec(memory_space=pltpu.VMEM),) * 2,
        scratch_shapes=scratch,
        compiler_params=pltpu.CompilerParams(
            collective_id=0, has_side_effects=True, vmem_limit_bytes=48 * 2**20
        ),
        name="solve",
    )(*operands)


def solution(mesh):
    sizes = [mesh.shape[name] for name in ("layer", "prow", "pcol")]
    return jax.shard_map(
        functools.partial(per_device, *sizes),
        mesh=mesh,
        in_specs=(
            P("layer", None, "prow", None, None),
            P("layer", None, "prow", None, None),
            P("layer", None, "pcol", None, None),
            P("layer", None, "prow", "pcol", None, None),
            P("layer", None, "prow", "pcol", None, None),
            P("layer", None, "prow", "pcol"),
            P("layer", None, None),
            P("prow", None, None),
            P("prow", None, None),
            P("prow", None, None),
            P("layer", "prow", "pcol", None, None),
            P("layer", "prow", "pcol", None, None),
            P("layer", "prow", "pcol"),
        ),
        out_specs=(P("layer", None, "pcol", None, None), P("prow", None, None)),
        check_vma=False,
    )
```

time: 761 us -> 90.9 us (0.12)
  waiting for transfers between devices: 576 us -> 0 us
  blocking collectives: 155 us -> 0 us
  Pallas kernels: 0 us -> 77 us
  between operations: 14 us -> 0.66 us
  local copies, waits for them, and re-layouts: 2.55 us -> 11.9 us
  matrix products: 7.68 us -> 0 us
    psum x3 -> x0, waiting for transfers between devices: 576 us -> none  [the longest x1 313 us: per_device(): anc_total = lax.psum(anc_partial, ('layer', 'pcol'))]
    psum x6 -> x0, blocking collectives: 98.7 us -> none  [the longest x3 50.9 us: broadcast(): return lax.psum(kept, axis)]
    pallas_call x0 -> x1, Pallas kernels: none -> 77 us  [per_device(): pl.pallas_call(functools.partial(kernel, nl, ny, nz, levels, rows, rq, S)...]
    all_gather x2 -> x0, blocking collectives: 56.7 us -> none  [per_device(): whole_level = lax.all_gather(column_rows, 'pcol', axis=0, tiled=True)]
    unnamed x24 -> x29, local copies, waits for them, and re-layouts: 0.51 us -> 11.9 us
    dot_general x13 -> x0, matrix products: 7.68 us -> none  [the longest x6 3.58 us: apply_inverse(): jnp.einsum('irs,ist->irt', lowered, inverse, preferred_element_type=jnp.f...]
  transfers between devices with their start and end apart: 3 -> 0, of which waited for: 3 -> 0; matrix products, arithmetic and copies ran while one was open for 0% -> 0% of each run, Pallas kernels for 0% -> 0%
where the time goes in v1:
time: 90.9 us; the launch traced here: 89.5 us
  Pallas kernels  77 us (85%)
  local copies, waits for them, and re-layouts  11.9 us (13%)
    pallas_call x1, Pallas kernels, per_device(): pl.pallas_call(functools.partial(kernel, nl, ny, nz, levels, rows, rq, S)...  77 us
    unnamed x29, local copies, waits for them, and re-layouts  11.9 us

profile of v1, /device:TPU:6, one launch (start us, length us, event | category | flops | bytes accessed | tf_op | source)
XLA Modules:
  0.0 89.5 jit_solution(977965413644753078)
XLA Ops:
  0.6 0.0 copy-start.11
  0.6 0.7 copy.16.sizes
  1.3 0.0 copy-done.11
  1.3 0.0 copy-start.10
  1.3 0.1 copy.17.anc_pattern
  1.4 0.6 copy-done.10
  2.0 0.1 copy.15.pattern
  2.1 0.0 copy-start
  2.1 1.0 %copy-done = bf16[1,3,4,128,128]{4,3,2,1,0:T(8,128)(2,1)S(1)} copy-done((bf16[1,3,4,128,128]{4,3,2,1,0:T(8,128)(2,1)S(1)}, bf16[1,3,4,128,128]{4,3,2,1,0:T(8,128)(2,1)}, u32[]{:S(2)}) %copy-start) | copy-done | bytes 393240
  3.1 0.0 copy-start.1
  3.1 0.9 %copy-done.1 = bf16[1,2,4,1,128,128]{5,4,3,2,1,0:T(8,128)(2,1)S(1)} copy-done((bf16[1,2,4,1,128,128]{5,4,3,2,1,0:T(8,128)(2,1)S(1)}, bf16[1,2,4,1,128,128]{5,4,3,2,1,0:T(8,128)(2,1)}, u32[]{:S(2)}) %copy-start.1) | copy-done | bytes 262168
  4.1 0.0 copy-start.2
  4.1 0.9 %copy-done.2 = bf16[1,2,4,1,128,128]{5,4,3,2,1,0:T(8,128)(2,1)S(1)} copy-done((bf16[1,2,4,1,128,128]{5,4,3,2,1,0:T(8,128)(2,1)S(1)}, bf16[1,2,4,1,128,128]{5,4,3,2,1,0:T(8,128)(2,1)}, u32[]{:S(2)}) %copy-start.2) | copy-done | bytes 262168
  5.0 0.0 copy-start.3
  5.0 0.9 %copy-done.3 = bf16[1,3,4,64,128]{4,3,2,1,0:T(8,128)(2,1)S(1)} copy-done((bf16[1,3,4,64,128]{4,3,2,1,0:T(8,128)(2,1)S(1)}, bf16[1,3,4,64,128]{4,3,2,1,0:T(8,128)(2,1)}, u32[]{:S(2)}) %copy-start.3) | copy-done | bytes 196632
  5.9 0.0 copy-start.4
  5.9 0.9 %copy-done.4 = bf16[4,128,128]{2,1,0:T(8,128)(2,1)S(1)} copy-done((bf16[4,128,128]{2,1,0:T(8,128)(2,1)S(1)}, bf16[4,128,128]{2,1,0:T(8,128)(2,1)}, u32[]{:S(2)}) %copy-start.4) | copy-done | bytes 131096
  6.8 0.0 copy-start.5
  6.8 0.9 %copy-done.5 = bf16[4,128,128]{2,1,0:T(8,128)(2,1)S(1)} copy-done((bf16[4,128,128]{2,1,0:T(8,128)(2,1)S(1)}, bf16[4,128,128]{2,1,0:T(8,128)(2,1)}, u32[]{:S(2)}) %copy-start.5) | copy-done | bytes 131096
  7.7 0.0 copy-start.6
  7.7 0.9 %copy-done.6 = bf16[1,4,1,128,128]{4,3,2,1,0:T(8,128)(2,1)S(1)} copy-done((bf16[1,4,1,128,128]{4,3,2,1,0:T(8,128)(2,1)S(1)}, bf16[1,4,1,128,128]{4,3,2,1,0:T(8,128)(2,1)}, u32[]{:S(2)}) %copy-start.6) | copy-done | bytes 131096
  8.6 0.0 copy-start.7
  8.7 0.9 %copy-done.7 = bf16[1,4,1,128,128]{4,3,2,1,0:T(8,128)(2,1)S(1)} copy-done((bf16[1,4,1,128,128]{4,3,2,1,0:T(8,128)(2,1)S(1)}, bf16[1,4,1,128,128]{4,3,2,1,0:T(8,128)(2,1)}, u32[]{:S(2)}) %copy-start.7) | copy-done | bytes 131096
  9.6 0.0 copy-start.8
  9.6 0.9 copy-done.8
  10.4 0.0 copy-start.9
  10.4 0.8 copy-done.9
  11.3 77.0 %solve.1 = (bf16[1,3,1,64,128]{4,3,2,1,0:T(8,128)(2,1)S(1)}, bf16[4,64,128]{2,1,0:T(8,128)(2,1)S(1)}) custom-call(bf16[1,3,4,64,128]{4,3,2,1,0:T(8,128)(2,1)S(1)} %copy-done.3, bf16[1,3,4,128,128]{4,3,2,1,0:T(8,128)(2,1)S(1)} %copy-done, bf16[1,3,1,128,128]{4,3,2,1,0:T(8,128)(2,1)S(1)} %copy-done.8, bf16[1,2,4,1,128,128]{5,4,3,2,1,0:T(8,128)(2,1)S(1)} %copy-done.1, ...), custom_call_target="tpu_custom_call" | custom-call | tf_op jit(solution)/shard_map/solve/pallas_call | solution.py:319
  88.3 0.6 copy.20
  88.9 0.6 copy.21
Async XLA Ops:
  0.6 0.7 copy-start.11
  1.3 0.7 copy-start.10
  2.1 1.0 %copy-start = (bf16[1,3,4,128,128]{4,3,2,1,0:T(8,128)(2,1)S(1)}, bf16[1,3,4,128,128]{4,3,2,1,0:T(8,128)(2,1)}, u32[]{:S(2)}) copy-start(bf16[1,3,4,128,128]{4,3,2,1,0:T(8,128)(2,1)} %diag_low.1) | copy-start | bytes 1179652
  3.1 0.9 %copy-start.1 = (bf16[1,2,4,1,128,128]{5,4,3,2,1,0:T(8,128)(2,1)S(1)}, bf16[1,2,4,1,128,128]{5,4,3,2,1,0:T(8,128)(2,1)}, u32[]{:S(2)}) copy-start(bf16[1,2,4,1,128,128]{5,4,3,2,1,0:T(8,128)(2,1)} %low.1) | copy-start | bytes 786436
  4.1 0.9 %copy-start.2 = (bf16[1,2,4,1,128,128]{5,4,3,2,1,0:T(8,128)(2,1)S(1)}, bf16[1,2,4,1,128,128]{5,4,3,2,1,0:T(8,128)(2,1)}, u32[]{:S(2)}) copy-start(bf16[1,2,4,1,128,128]{5,4,3,2,1,0:T(8,128)(2,1)} %up.1) | copy-start | bytes 786436
  5.0 0.9 %copy-start.3 = (bf16[1,3,4,64,128]{4,3,2,1,0:T(8,128)(2,1)S(1)}, bf16[1,3,4,64,128]{4,3,2,1,0:T(8,128)(2,1)}, u32[]{:S(2)}) copy-start(bf16[1,3,4,64,128]{4,3,2,1,0:T(8,128)(2,1)} %rhs.1) | copy-start | bytes 589828
  5.9 0.9 %copy-start.4 = (bf16[4,128,128]{2,1,0:T(8,128)(2,1)S(1)}, bf16[4,128,128]{2,1,0:T(8,128)(2,1)}, u32[]{:S(2)}) copy-start(bf16[4,128,128]{2,1,0:T(8,128)(2,1)} %anc_dl.1) | copy-start | bytes 393220
  6.8 0.9 %copy-start.5 = (bf16[4,128,128]{2,1,0:T(8,128)(2,1)S(1)}, bf16[4,128,128]{2,1,0:T(8,128)(2,1)}, u32[]{:S(2)}) copy-start(bf16[4,128,128]{2,1,0:T(8,128)(2,1)} %anc_du.1) | copy-start | bytes 393220
  7.7 0.9 %copy-start.6 = (bf16[1,4,1,128,128]{4,3,2,1,0:T(8,128)(2,1)S(1)}, bf16[1,4,1,128,128]{4,3,2,1,0:T(8,128)(2,1)}, u32[]{:S(2)}) copy-start(bf16[1,4,1,128,128]{4,3,2,1,0:T(8,128)(2,1)} %anc_low.1) | copy-start | bytes 393220
  8.6 0.9 %copy-start.7 = (bf16[1,4,1,128,128]{4,3,2,1,0:T(8,128)(2,1)S(1)}, bf16[1,4,1,128,128]{4,3,2,1,0:T(8,128)(2,1)}, u32[]{:S(2)}) copy-start(bf16[1,4,1,128,128]{4,3,2,1,0:T(8,128)(2,1)} %anc_up.1) | copy-start | bytes 393220
  9.6 0.9 copy-start.8
  10.4 0.8 copy-start.9

commit v2 on v1

--- a/solution.py
+++ b/solution.py
@@ -94,10 +94,10 @@
 
     def link(n, i):
         if n < levels - 1:
-            return pat_v[0, n, i, 0]
+            return pat_v[0, n, 0, i]
         if n < levels + 1:
-            return apat_v[0, i, 0]
-        return pat_v[0, nset - 1 - n, i, 0]
+            return apat_v[0, 0, i]
+        return pat_v[0, nset - 1 - n, 0, i]
 
     def mask_set(n):
         got_sets[n].wait()
@@ -124,7 +124,7 @@
 
     def live(level, value):
         columns = lax.broadcasted_iota(jnp.int32, value.shape, 1)
-        return jnp.where(columns < size_v[0, level, c], value, 0.0).astype(BF16)
+        return jnp.where(columns < size_v[level, 0, c], value, 0.0).astype(BF16)
 
     got_pat.wait()
     got_apat.wait()
@@ -288,8 +288,11 @@
 
 
 def per_device(nl, ny, nz, *operands):
-    rhs, diag_low = operands[0], operands[1]
-    anc_rhs = operands[7]
+    operands = list(operands)
+    operands[5] = operands[5].transpose(0, 1, 3, 2)
+    operands[6] = operands[6].transpose(1, 0, 2)
+    operands[12] = operands[12].transpose(0, 2, 1)
+    rhs = operands[0]
     levels, rows, R, S = rhs.shape[1:]
     rq = R // ny
     nset = 2 * levels
@@ -326,7 +329,7 @@
         out_specs=(pl.BlockSpec(memory_space=pltpu.VMEM),) * 2,
         scratch_shapes=scratch,
         compiler_params=pltpu.CompilerParams(
-            collective_id=0, has_side_effects=True, vmem_limit_bytes=48 * 2**20
+            collective_id=0, has_side_effects=True, vmem_limit_bytes=60 * 2**20
         ),
         name="solve",
     )(*operands)

time: 90.9 us -> 81.5 us (0.90)
  local copies, waits for them, and re-layouts: 11.9 us -> 2.09 us
    unnamed x29 -> x4, local copies, waits for them, and re-layouts: 11.9 us -> 2.09 us
where the time goes in v2:
time: 81.5 us; the launch traced here: 80.4 us
  Pallas kernels  77.6 us (95%)
  local copies, waits for them, and re-layouts  2.09 us (3%)
    pallas_call x1, Pallas kernels, per_device(): pl.pallas_call(functools.partial(kernel, nl, ny, nz, levels, rows, rq, S)...  77.6 us
    unnamed x4, local copies, waits for them, and re-layouts  2.09 us

profile of v2, /device:TPU:6, one launch (start us, length us, event | category | flops | bytes accessed | tf_op | source)
XLA Modules:
  0.0 80.4 jit_solution(9426852241807057290)
XLA Ops:
  0.6 77.6 %solve.1 = (bf16[1,3,1,64,128]{4,3,2,1,0:T(8,128)(2,1)}, bf16[4,64,128]{2,1,0:T(8,128)(2,1)}) custom-call(bf16[1,3,4,64,128]{4,3,2,1,0:T(8,128)(2,1)} %rhs.1, bf16[1,3,4,128,128]{4,3,2,1,0:T(8,128)(2,1)} %diag_low.1, bf16[1,3,1,128,128]{4,3,2,1,0:T(8,128)(2,1)} %diag_up.1, bf16[1,2,4,1,128,128]{5,4,3,2,1,0:T(8,128)(2,1)} %low.1, ...), custom_call_target="tpu_custom_call" | custom-call | tf_op jit(solution)/shard_map/solve/pallas_call | solution.py:322
  78.3 0.0 copy-start
  78.3 1.5 %copy.18 = bf16[1,3,1,64,128]{4,3,2,1,0:T(8,128)(2,1)} copy(bf16[1,3,1,64,128]{4,3,2,1,0:T(8,128)(2,1)} %get-tuple-element.4) | data formatting | bytes 98304
  79.7 0.0 copy-done
  79.8 0.6 copy.19
Async XLA Ops:
  78.3 1.5 %copy-start = (bf16[4,64,128]{2,1,0:T(8,128)(2,1)S(1)}, bf16[4,64,128]{2,1,0:T(8,128)(2,1)}, u32[]{:S(2)}) copy-start(bf16[4,64,128]{2,1,0:T(8,128)(2,1)} %get-tuple-element.5) | copy-start | bytes 196612

commit v3 on v2

--- a/solution.py
+++ b/solution.py
@@ -27,9 +27,10 @@
     osol, oanc,
     pat_v, apat_v, size_v, raw, dmine, rfull, f0, dup, quarter,
     fset, bset,
-    fsrc, frecv, lrecv, ag, final,
+    fsrc, frecv, lrecv, ag, wg, ring, eacc,
     in_sem, own_sem, far_sem, set_send, set_recv, one_send, one_recv,
     fs_sem, fr_sem, l_send, l_recv, ag_send, ag_recv, oa_send, oa_recv, os_send, os_recv,
+    w_send, w_recv, ring_send, ring_recv,
 ):
     k = lax.axis_index("layer")
     p = lax.axis_index("prow")
@@ -37,6 +38,9 @@
     j = lax.rem(c, rows)
     owner = p == c // rows
     nset = 2 * levels
+    composed = nset
+    ring_steps = nz // 2
+    half = rows * S // 2
     y_order, z_order, l_order = far_first(ny), far_first(nz), far_first(nl)
 
     def y_peer(d):
@@ -126,6 +130,36 @@
         columns = lax.broadcasted_iota(jnp.int32, value.shape, 1)
         return jnp.where(columns < size_v[level, 0, c], value, 0.0).astype(BF16)
 
+    def ring_parts(t, h, move):
+        both = [(0, lax.rem(c + nz - t - move, nz), 1), (1, lax.rem(c + t + move, nz), nz - 1)]
+        return [both[h]] if t == ring_steps - 1 else both
+
+    ring_copies = []
+
+    def ring_start(t, h):
+        for m, slot, d in ring_parts(t, h, 0):
+            block = ring.at[slot, pl.ds(h * half, half)]
+            copy = remote(block, block, ring_send.at[m, h, t], ring_recv.at[m, h, t], z_peer(d))
+            copy.start()
+            ring_copies.append(copy)
+
+    def ring_pass(t):
+        for h in range(2):
+            for m, slot, d in ring_parts(t, h, 1):
+                drain(ring.at[slot, pl.ds(h * half, half)], ring_recv.at[m, h, t])
+            if t + 1 < ring_steps:
+                ring_start(t + 1, h)
+
+    def up0(slot):
+        row = pl.ds(pl.multiple_of(lax.rem(slot, rows) * S, S), S)
+        return bset[levels - 1, slot // rows, row, :]
+
+    def compose(offsets):
+        slots = [lax.rem(c + o, nz) for o in offsets]
+        left = jnp.concatenate([ring[slot] for slot in slots], axis=1)
+        right = jnp.concatenate([up0(slot) for slot in slots], axis=0)
+        eacc[...] += dot(left, right)
+
     got_pat.wait()
     got_apat.wait()
     got_size.wait()
@@ -141,6 +175,10 @@
         for n in range(levels):
             quarter[n + 1] = rfull[n + 1, mine]
 
+    eacc[...] = jnp.zeros_like(eacc)
+    mask_set(levels + 1)
+    got_dup.wait()
+    ring[c] = live(1, dot(bset[1, p], dup[1]))
     pl.semaphore_wait(barrier, len(greeted))
     for d in (reach, nz - reach):
         pl.semaphore_signal(far_sem, inc=1, device_id=z_peer(d), device_id_type=MESH)
@@ -173,6 +211,8 @@
 
     send_one(0)
     send_set(0)
+    ring_start(0, 0)
+    ring_start(0, 1)
     send_one(1)
     send_one(2)
     mask_set(1)
@@ -184,9 +224,29 @@
             copy.wait()
 
     send_one(3)
-    for n in range(2, nset):
-        mask_set(n)
+
+    for n in [2, nset - 1, levels, levels + 1]:
+        if n != levels + 1:
+            mask_set(n)
         send_set(n)
+    ring_pass(0)
+    if ring_steps > 1:
+        ring_pass(1)
+
+    plan = {
+        1: [("step", 2)],
+        2: [("step", 3)],
+        3: [("step", 4), ("add", 1), ("add", 2), ("add", 3), ("add", 4)],
+        4: [("step", 5)],
+        5: [("step", 6), ("add", 5), ("add", 6), ("step", 7), ("add", 7)],
+    }
+
+    def background(phase):
+        for what, n in plan[phase]:
+            if what == "step" and n < ring_steps:
+                ring_pass(n)
+            if what == "add" and n < ring_steps:
+                compose([n, nz - n])
 
     segment = None
     forward = []
@@ -212,6 +272,12 @@
             wait_one(2)
         if level == 2:
             wait_one(3)
+            wg[c] = live(1, dot(segment, dup[1]))
+            for d in z_order:
+                remote(wg.at[c], wg.at[c], w_send, w_recv, z_peer(d)).start()
+        if level == levels:
+            wait_set(nset - 1)
+        background(level)
         drain(frecv.at[n], fr_sem.at[n])
         total = fsrc[n, c].astype(F32)
         for d in range(1, nz):
@@ -224,6 +290,7 @@
     lrecv[k] = total.astype(BF16)
     for d in l_order:
         remote(lrecv.at[k], lrecv.at[k], l_send, l_recv, l_peer(d)).start()
+    background(4)
     drain(lrecv.at[pl.ds(0, nl - 1)], l_recv)
     total = lrecv[0].astype(F32)
     for n in range(1, nl):
@@ -233,46 +300,65 @@
     solved = dot(afwd, dmine[levels + 1]).astype(BF16)
 
     mine = pl.ds(pl.multiple_of(p * rq, rq), rq)
-    got_dup.wait()
     sol_copies = []
     anc_copies = []
-    for step in range(levels + 1):
-        level = levels - step
-        if level < levels:
-            osol[0, level, 0, mine] = solved
-            part = osol.at[0, level, 0, mine]
-            for m, d in enumerate(y_order):
-                copy = remote(part, part, os_send.at[level, m], os_recv.at[level], y_peer(d))
-                copy.start()
-                sol_copies.append(copy)
-        if level == 0:
-            break
-        ag[step, c] = solved
+
+    def give(level, value):
+        osol[0, level, 0, mine] = value
+        part = osol.at[0, level, 0, mine]
+        for m, d in enumerate(y_order):
+            copy = remote(part, part, os_send.at[level, m], os_recv.at[level], y_peer(d))
+            copy.start()
+            sol_copies.append(copy)
+
+    def spread(step, value):
+        ag[step, c] = value
         for d in z_order:
             remote(ag.at[step, c], ag.at[step, c], ag_send.at[step], ag_recv.at[step], z_peer(d)).start()
-        wait_set(levels + step)
-        drain(ag.at[step, pl.ds(0, nz - 1)], ag_recv.at[step])
-        if step == 0:
-            for i in range(rows):
-                oanc[i, mine] = ag[0, p * rows + i]
-                for m, d in enumerate(y_order):
-                    theirs = lax.rem(p + d, ny) * rows + i
-                    copy = remote(ag.at[0, theirs], oanc.at[i, mine], oa_send.at[i, m], oa_recv, y_peer(d))
-                    copy.start()
-                    anc_copies.append(copy)
+
+    def parents(slots, s):
+        return jnp.concatenate([slots[s * rows + i] for i in range(rows)], axis=1)
+
+    def sums(slots, blocks):
         total = None
         for s in range(ny):
-            parents = jnp.concatenate([ag[step, s * rows + i] for i in range(rows)], axis=1)
-            product = dot(parents, bset[step, s])
+            product = dot(parents(slots, s), blocks[s])
             total = product if total is None else total + product
-        below = level - 1
-        lowered = (forward[below].astype(F32) - total).astype(BF16)
-        solved = live(below, dot(lowered, dup[below]))
+        return total
+
+    def finish(level, total):
+        lowered = (forward[level].astype(F32) - total).astype(BF16)
+        return live(level, dot(lowered, dup[level]))
+
+    spread(0, solved)
+    background(5)
+    compose([0, nz // 2])
+    bset[levels, p] = eacc[...].astype(BF16)
+    send_set(composed)
+    drain(wg.at[pl.ds(0, nz - 1)], w_recv)
+    fixed = sums(wg, bset.at[levels - 1])
+    wait_set(levels)
+    drain(ag.at[0, pl.ds(0, nz - 1)], ag_recv.at[0])
+    top = finish(levels - 1, sums(ag.at[0], bset.at[0]))
+    spread(1, top)
+    give(levels - 1, top)
+    for i in range(rows):
+        oanc[i, mine] = ag[0, p * rows + i]
+        for m, d in enumerate(y_order):
+            theirs = lax.rem(p + d, ny) * rows + i
+            copy = remote(ag.at[0, theirs], oanc.at[i, mine], oa_send.at[i, m], oa_recv, y_peer(d))
+            copy.start()
+            anc_copies.append(copy)
+    wait_set(levels + 1)
+    wait_set(composed)
+    drain(ag.at[1, pl.ds(0, nz - 1)], ag_recv.at[1])
+    give(0, finish(0, fixed - sums(ag.at[1], bset.at[levels])))
+    give(1, finish(1, sums(ag.at[1], bset.at[1])))
 
     for level in reversed(range(levels)):
         drain(osol.at[0, level, 0, pl.ds(0, (ny - 1) * rq)], os_recv.at[level])
     drain(oanc.at[:, pl.ds(0, (ny - 1) * rq)], oa_recv)
-    for copy in set_copies + sol_copies + anc_copies:
+    for copy in set_copies + sol_copies + anc_copies + ring_copies:
         copy.wait_send()
 
     @pl.when(owner)
@@ -283,7 +369,9 @@
 
     for n in range(levels):
         drain(frecv.at[n], fs_sem.at[n])
+    for n in range(2):
         drain(ag.at[n, pl.ds(0, nz - 1)], ag_send.at[n])
+    drain(wg.at[pl.ds(0, nz - 1)], w_send)
     drain(lrecv.at[pl.ds(0, nl - 1)], l_send)
 
 
@@ -308,16 +396,19 @@
         pltpu.VMEM((levels, S, S), BF16),
         pltpu.VMEM((levels + 1, rq, S), BF16),
         pltpu.VMEM((levels, ny, S, rows * S), BF16),
-        pltpu.VMEM((levels, ny, rows * S, S), BF16),
+        pltpu.VMEM((levels + 1, ny, rows * S, S), BF16),
         pltpu.VMEM((levels, nz, rq, S), BF16),
         pltpu.VMEM((levels, nz - 1, rq, S), BF16),
         pltpu.VMEM((nl, rq, S), BF16),
-        pltpu.VMEM((levels, nz, rq, S), BF16),
-        pltpu.VMEM((rq, S), BF16),
+        pltpu.VMEM((2, nz, rq, S), BF16),
+        pltpu.VMEM((nz, rq, S), BF16),
+        pltpu.VMEM((nz, rows * S, S), BF16),
+        pltpu.VMEM((rows * S, S), F32),
         dma((4 + nset,)), dma((5,)), pltpu.SemaphoreType.REGULAR,
-        dma((nset, ny - 1)), dma((nset,)), dma((4, ny - 1)), dma((4,)),
-        dma((levels,)), dma((levels,)), dma, dma, dma((levels,)), dma((levels,)),
+        dma((nset + 1, ny - 1)), dma((nset + 1,)), dma((4, ny - 1)), dma((4,)),
+        dma((levels,)), dma((levels,)), dma, dma, dma((2,)), dma((2,)),
         dma((rows, ny - 1)), dma, dma((levels, ny - 1)), dma((levels,)),
+        dma, dma, dma((2, 2, nz // 2)), dma((2, 2, nz // 2)),
     ]
     return pl.pallas_call(
         functools.partial(kernel, nl, ny, nz, levels, rows, rq, S),

time: 81.5 us -> 77 us (0.945); the launches traced: 80.4 us -> 76.8 us
  Pallas kernels: 77.6 us -> 74.1 us
    pallas_call x1, Pallas kernels: 77.6 us -> 74.1 us  [per_device(): pl.pallas_call(functools.partial(kernel, nl, ny, nz, levels, rows, rq, S)...]
where the time goes in v3:
time: 77 us; the launch traced here: 76.8 us
  Pallas kernels  74.1 us (96%)
  local copies, waits for them, and re-layouts  2.09 us (3%)
    pallas_call x1, Pallas kernels, per_device(): pl.pallas_call(functools.partial(kernel, nl, ny, nz, levels, rows, rq, S)...  74.1 us
    unnamed x4, local copies, waits for them, and re-layouts  2.09 us

profile of v3, /device:TPU:6, one launch (start us, length us, event | category | flops | bytes accessed | tf_op | source)
XLA Modules:
  0.0 76.8 jit_solution(14808995436863779120)
XLA Ops:
  0.6 74.1 %solve.1 = (bf16[1,3,1,64,128]{4,3,2,1,0:T(8,128)(2,1)}, bf16[4,64,128]{2,1,0:T(8,128)(2,1)}) custom-call(bf16[1,3,4,64,128]{4,3,2,1,0:T(8,128)(2,1)} %rhs.1, bf16[1,3,4,128,128]{4,3,2,1,0:T(8,128)(2,1)} %diag_low.1, bf16[1,3,1,128,128]{4,3,2,1,0:T(8,128)(2,1)} %diag_up.1, bf16[1,2,4,1,128,128]{5,4,3,2,1,0:T(8,128)(2,1)} %low.1, ...), custom_call_target="tpu_custom_call" | custom-call | tf_op jit(solution)/shard_map/solve/pallas_call | solution.py:413
  74.7 0.0 copy-start
  74.7 1.5 %copy.18 = bf16[1,3,1,64,128]{4,3,2,1,0:T(8,128)(2,1)} copy(bf16[1,3,1,64,128]{4,3,2,1,0:T(8,128)(2,1)} %get-tuple-element.4) | data formatting | bytes 98304
  76.2 0.0 copy-done
  76.2 0.6 copy.19
Async XLA Ops:
  74.7 1.5 %copy-start = (bf16[4,64,128]{2,1,0:T(8,128)(2,1)S(1)}, bf16[4,64,128]{2,1,0:T(8,128)(2,1)}, u32[]{:S(2)}) copy-start(bf16[4,64,128]{2,1,0:T(8,128)(2,1)} %get-tuple-element.5) | copy-start | bytes 196612

commit v4 on v3

--- a/solution.py
+++ b/solution.py
@@ -25,10 +25,10 @@
     rhs, diag_low, diag_up, low, up, pattern, sizes,
     anc_rhs, anc_dl, anc_du, anc_low, anc_up, anc_pattern,
     osol, oanc,
-    pat_v, apat_v, size_v, raw, dmine, rfull, f0, dup, quarter,
+    pat_v, apat_v, size_v, raw, dmine, rfull, f0, dup, quarter, amat, afull, arhs,
     fset, bset,
-    fsrc, frecv, lrecv, ag, wg, ring, eacc,
-    in_sem, own_sem, far_sem, set_send, set_recv, one_send, one_recv,
+    fsrc, frecv, asrc, arecv, lrecv, agx, ag, wg, ring, eacc,
+    in_sem, own_sem, anc_in, far_sem, set_send, set_recv, one_send, one_recv, anc_send, anc_recv,
     fs_sem, fr_sem, l_send, l_recv, ag_send, ag_recv, oa_send, oa_recv, os_send, os_recv,
     w_send, w_recv, ring_send, ring_recv,
 ):
@@ -39,6 +39,8 @@
     owner = p == c // rows
     nset = 2 * levels
     composed = nset
+    zh = nz // 2
+    g = lax.rem(c, zh)
     ring_steps = nz // 2
     half = rows * S // 2
     y_order, z_order, l_order = far_first(ny), far_first(nz), far_first(nl)
@@ -82,15 +84,28 @@
     own = [
         pltpu.make_async_copy(diag_low.at[0, :, j], dmine.at[pl.ds(0, levels)], own_sem.at[0]),
         pltpu.make_async_copy(rhs.at[0, :, j], rfull.at[pl.ds(0, levels)], own_sem.at[1]),
-        pltpu.make_async_copy(anc_rhs.at[j], rfull.at[levels], own_sem.at[2]),
-        pltpu.make_async_copy(anc_dl.at[j], dmine.at[levels], own_sem.at[3]),
-        pltpu.make_async_copy(anc_du.at[j], dmine.at[levels + 1], own_sem.at[4]),
+    ]
+    holder = [p == (g + u * zh) // rows for u in range(2)]
+    anc_row = [lax.rem(g + u * zh, rows) for u in range(2)]
+    anc_own = [
+        [
+            pltpu.make_async_copy(anc_rhs.at[anc_row[u]], afull.at[u], anc_in.at[u, 0]),
+            pltpu.make_async_copy(anc_dl.at[anc_row[u]], amat.at[u, 0], anc_in.at[u, 1]),
+            pltpu.make_async_copy(anc_du.at[anc_row[u]], amat.at[u, 1], anc_in.at[u, 2]),
+        ]
+        for u in range(2)
     ]
 
     @pl.when(owner)
     def _():
         for copy in own:
             copy.start()
+
+    for u in range(2):
+        @pl.when(holder[u])
+        def _():
+            for copy in anc_own[u]:
+                copy.start()
 
     for n in range(1, nset):
         got_sets.append(fetch(sets_in[n], raw.at[n], 3 + n))
@@ -167,13 +182,13 @@
 
     @pl.when(owner)
     def _():
-        for copy in own[:3]:
+        for copy in own:
             copy.wait()
         f0[...] = live(0, dot(rfull[0], dmine[0]))
         mine = pl.ds(pl.multiple_of(p * rq, rq), rq)
         quarter[0] = f0[mine]
-        for n in range(levels):
-            quarter[n + 1] = rfull[n + 1, mine]
+        for n in range(1, levels):
+            quarter[n] = rfull[n, mine]
 
     eacc[...] = jnp.zeros_like(eacc)
     mask_set(levels + 1)
@@ -187,9 +202,9 @@
         theirs = pl.ds(pl.multiple_of(lax.rem(p + d, ny) * rq, rq), rq)
         pairs = [
             (f0.at[theirs], quarter.at[0]),
-            (rfull.at[pl.ds(1, levels), theirs], quarter.at[pl.ds(1, levels)]),
+            (rfull.at[pl.ds(1, levels - 1), theirs], quarter.at[pl.ds(1, levels - 1)]),
             (dmine.at[1], dmine.at[1]),
-            (dmine.at[pl.ds(2, levels)], dmine.at[pl.ds(2, levels)]),
+            (dmine.at[pl.ds(2, levels - 2)], dmine.at[pl.ds(2, levels - 2)]),
         ]
         return [
             remote(src, dst, one_send.at[n, m], one_recv.at[n], y_peer(d))
@@ -218,14 +233,30 @@
     mask_set(1)
     send_set(1)
 
-    @pl.when(owner)
-    def _():
-        for copy in own[3:]:
-            copy.wait()
-
     send_one(3)
 
-    for n in [2, nset - 1, levels, levels + 1]:
+    def anc_copies_of(u, m, d):
+        theirs = pl.ds(pl.multiple_of(lax.rem(p + d, ny) * rq, rq), rq)
+        return [
+            remote(afull.at[u, theirs], arhs.at[u], anc_send.at[u, 0, m], anc_recv.at[u, 0], y_peer(d)),
+            remote(amat.at[u], amat.at[u], anc_send.at[u, 1, m], anc_recv.at[u, 1], y_peer(d)),
+        ]
+
+    anc_given = [[anc_copies_of(u, m, d) for m, d in enumerate(y_order)] for u in range(2)]
+
+    mask_set(2)
+    send_set(2)
+    for u in range(2):
+        @pl.when(holder[u])
+        def _():
+            for copy in anc_own[u]:
+                copy.wait()
+            arhs[u] = afull[u, pl.ds(pl.multiple_of(p * rq, rq), rq)]
+            for copies in anc_given[u]:
+                for copy in copies:
+                    copy.start()
+
+    for n in [nset - 1, levels, levels + 1]:
         if n != levels + 1:
             mask_set(n)
         send_set(n)
@@ -238,7 +269,8 @@
         2: [("step", 3)],
         3: [("step", 4), ("add", 1), ("add", 2), ("add", 3), ("add", 4)],
         4: [("step", 5)],
-        5: [("step", 6), ("add", 5), ("add", 6), ("step", 7), ("add", 7)],
+        5: [("step", 6), ("add", 5), ("add", 6)],
+        6: [("step", 7), ("add", 7)],
     }
 
     def background(phase):
@@ -261,12 +293,21 @@
         for s in range(ny):
             product = dot(segment, fset[n, s])
             for i in range(rows):
-                fsrc[n, s * rows + i] = product[:, i * S:(i + 1) * S].astype(BF16)
+                piece = product[:, i * S:(i + 1) * S].astype(BF16)
+                row = s * rows + i
+                if level < levels:
+                    fsrc[n, row] = piece
+                else:
+                    asrc[row % zh, row // zh] = piece
         if n == 0:
             pl.semaphore_wait(far_sem, 2)
         for d in z_order:
             target = lax.rem(c + d, nz)
-            remote(fsrc.at[n, target], frecv.at[n, d - 1], fs_sem.at[n], fr_sem.at[n], z_peer(d)).start()
+            if level < levels:
+                src, dst = fsrc.at[n, target], frecv.at[n, d - 1]
+            else:
+                src, dst = asrc.at[lax.rem(target, zh)], arecv.at[c]
+            remote(src, dst, fs_sem.at[n], fr_sem.at[n], z_peer(d)).start()
         if level == 1:
             wait_one(1)
             wait_one(2)
@@ -278,26 +319,38 @@
         if level == levels:
             wait_set(nset - 1)
         background(level)
+        if level == levels:
+            break
         drain(frecv.at[n], fr_sem.at[n])
         total = fsrc[n, c].astype(F32)
         for d in range(1, nz):
             total = total + frecv[n, d - 1].astype(F32)
-        if level < levels:
-            lowered = (quarter[level].astype(F32) - total).astype(BF16)
-            segment = live(level, dot(lowered, dmine[level]))
-            forward.append(segment)
-
+        lowered = (quarter[level].astype(F32) - total).astype(BF16)
+        segment = live(level, dot(lowered, dmine[level]))
+        forward.append(segment)
+
+    arecv[c] = asrc[g]
+    drain(arecv.at[pl.ds(0, nz - 1)], fr_sem.at[levels - 1])
+    total = arecv[0].astype(F32)
+    for n in range(1, nz):
+        total = total + arecv[n].astype(F32)
     lrecv[k] = total.astype(BF16)
     for d in l_order:
         remote(lrecv.at[k], lrecv.at[k], l_send, l_recv, l_peer(d)).start()
     background(4)
+    for u in range(2):
+        @pl.when(jnp.logical_not(holder[u]))
+        def _():
+            for copy in anc_given[u][0]:
+                copy.wait_recv()
     drain(lrecv.at[pl.ds(0, nl - 1)], l_recv)
     total = lrecv[0].astype(F32)
     for n in range(1, nl):
         total = total + lrecv[n].astype(F32)
-    lowered = (quarter[levels].astype(F32) - total).astype(BF16)
-    afwd = dot(lowered, dmine[levels]).astype(BF16)
-    solved = dot(afwd, dmine[levels + 1]).astype(BF16)
+    for u in range(2):
+        lowered = (arhs[u].astype(F32) - total[u]).astype(BF16)
+        afwd = dot(lowered, amat[u, 0]).astype(BF16)
+        agx[g, u] = dot(afwd, amat[u, 1]).astype(BF16)
 
     mine = pl.ds(pl.multiple_of(p * rq, rq), rq)
     sol_copies = []
@@ -311,18 +364,10 @@
             copy.start()
             sol_copies.append(copy)
 
-    def spread(step, value):
-        ag[step, c] = value
-        for d in z_order:
-            remote(ag.at[step, c], ag.at[step, c], ag_send.at[step], ag_recv.at[step], z_peer(d)).start()
-
-    def parents(slots, s):
-        return jnp.concatenate([slots[s * rows + i] for i in range(rows)], axis=1)
-
     def sums(slots, blocks):
         total = None
         for s in range(ny):
-            product = dot(parents(slots, s), blocks[s])
+            product = dot(jnp.concatenate(slots[s * rows:(s + 1) * rows], axis=1), blocks[s])
             total = product if total is None else total + product
         return total
 
@@ -330,30 +375,40 @@
         lowered = (forward[level].astype(F32) - total).astype(BF16)
         return live(level, dot(lowered, dup[level]))
 
-    spread(0, solved)
+    part = agx.at[g]
+    for d in sorted([d for d in range(1 - zh // 2, zh // 2 + 1) if d], key=lambda d: -abs(d)):
+        remote(part, part, ag_send.at[0], ag_recv.at[0], z_peer(d % nz)).start()
     background(5)
+    wait_set(levels)
+    drain(agx.at[pl.ds(0, zh - 1)], ag_recv.at[0])
+    top = finish(levels - 1, sums([agx[a % zh, a // zh] for a in range(nz)], bset.at[0]))
+    ag[c] = top
+    for d in z_order:
+        remote(ag.at[c], ag.at[c], ag_send.at[1], ag_recv.at[1], z_peer(d)).start()
+    background(6)
     compose([0, nz // 2])
     bset[levels, p] = eacc[...].astype(BF16)
     send_set(composed)
-    drain(wg.at[pl.ds(0, nz - 1)], w_recv)
-    fixed = sums(wg, bset.at[levels - 1])
-    wait_set(levels)
-    drain(ag.at[0, pl.ds(0, nz - 1)], ag_recv.at[0])
-    top = finish(levels - 1, sums(ag.at[0], bset.at[0]))
-    spread(1, top)
     give(levels - 1, top)
     for i in range(rows):
-        oanc[i, mine] = ag[0, p * rows + i]
+        row = p * rows + i
+        oanc[i, mine] = agx[lax.rem(row, zh), row // zh]
         for m, d in enumerate(y_order):
             theirs = lax.rem(p + d, ny) * rows + i
-            copy = remote(ag.at[0, theirs], oanc.at[i, mine], oa_send.at[i, m], oa_recv, y_peer(d))
+            copy = remote(
+                agx.at[lax.rem(theirs, zh), theirs // zh], oanc.at[i, mine], oa_send.at[i, m], oa_recv, y_peer(d),
+            )
             copy.start()
             anc_copies.append(copy)
+    drain(wg.at[pl.ds(0, nz - 1)], w_recv)
+    fixed = sums([wg[i] for i in range(nz)], bset.at[levels - 1])
     wait_set(levels + 1)
+    drain(ag.at[pl.ds(0, nz - 1)], ag_recv.at[1])
+    slots = [ag[i] for i in range(nz)]
+    second = finish(1, sums(slots, bset.at[1]))
     wait_set(composed)
-    drain(ag.at[1, pl.ds(0, nz - 1)], ag_recv.at[1])
-    give(0, finish(0, fixed - sums(ag.at[1], bset.at[levels])))
-    give(1, finish(1, sums(ag.at[1], bset.at[1])))
+    give(0, finish(0, fixed - sums(slots, bset.at[levels])))
+    give(1, second)
 
     for level in reversed(range(levels)):
         drain(osol.at[0, level, 0, pl.ds(0, (ny - 1) * rq)], os_recv.at[level])
@@ -367,10 +422,18 @@
             for copy in copies:
                 copy.wait_send()
 
-    for n in range(levels):
+    for u in range(2):
+        @pl.when(holder[u])
+        def _():
+            for copies in anc_given[u]:
+                for copy in copies:
+                    copy.wait_send()
+
+    for n in range(levels - 1):
         drain(frecv.at[n], fs_sem.at[n])
-    for n in range(2):
-        drain(ag.at[n, pl.ds(0, nz - 1)], ag_send.at[n])
+    drain(arecv.at[pl.ds(0, nz - 1)], fs_sem.at[levels - 1])
+    drain(agx.at[pl.ds(0, zh - 1)], ag_send.at[0])
+    drain(ag.at[pl.ds(0, nz - 1)], ag_send.at[1])
     drain(wg.at[pl.ds(0, nz - 1)], w_send)
     drain(lrecv.at[pl.ds(0, nl - 1)], l_send)
 
@@ -390,22 +453,29 @@
         pltpu.SMEM(operands[12].shape, jnp.int32),
         pltpu.SMEM(operands[6].shape, jnp.int32),
         pltpu.VMEM((nset, rows, S, S), BF16),
-        pltpu.VMEM((levels + 2, S, S), BF16),
-        pltpu.VMEM((levels + 1, R, S), BF16),
+        pltpu.VMEM((levels, S, S), BF16),
+        pltpu.VMEM((levels, R, S), BF16),
         pltpu.VMEM((R, S), BF16),
         pltpu.VMEM((levels, S, S), BF16),
-        pltpu.VMEM((levels + 1, rq, S), BF16),
+        pltpu.VMEM((levels, rq, S), BF16),
+        pltpu.VMEM((2, 2, S, S), BF16),
+        pltpu.VMEM((2, R, S), BF16),
+        pltpu.VMEM((2, rq, S), BF16),
         pltpu.VMEM((levels, ny, S, rows * S), BF16),
         pltpu.VMEM((levels + 1, ny, rows * S, S), BF16),
-        pltpu.VMEM((levels, nz, rq, S), BF16),
-        pltpu.VMEM((levels, nz - 1, rq, S), BF16),
-        pltpu.VMEM((nl, rq, S), BF16),
-        pltpu.VMEM((2, nz, rq, S), BF16),
+        pltpu.VMEM((levels - 1, nz, rq, S), BF16),
+        pltpu.VMEM((levels - 1, nz - 1, rq, S), BF16),
+        pltpu.VMEM((nz // 2, 2, rq, S), BF16),
+        pltpu.VMEM((nz, 2, rq, S), BF16),
+        pltpu.VMEM((nl, 2, rq, S), BF16),
+        pltpu.VMEM((nz // 2, 2, rq, S), BF16),
+        pltpu.VMEM((nz, rq, S), BF16),
         pltpu.VMEM((nz, rq, S), BF16),
         pltpu.VMEM((nz, rows * S, S), BF16),
         pltpu.VMEM((rows * S, S), F32),
-        dma((4 + nset,)), dma((5,)), pltpu.SemaphoreType.REGULAR,
+        dma((4 + nset,)), dma((2,)), dma((2, 3)), pltpu.SemaphoreType.REGULAR,
         dma((nset + 1, ny - 1)), dma((nset + 1,)), dma((4, ny - 1)), dma((4,)),
+        dma((2, 2, ny - 1)), dma((2, 2)),
         dma((levels,)), dma((levels,)), dma, dma, dma((2,)), dma((2,)),
         dma((rows, ny - 1)), dma, dma((levels, ny - 1)), dma((levels,)),
         dma, dma, dma((2, 2, nz // 2)), dma((2, 2, nz // 2)),
@@ -413,8 +483,8 @@
     return pl.pallas_call(
         functools.partial(kernel, nl, ny, nz, levels, rows, rq, S),
         out_shape=(
-            jax.ShapeDtypeStruct((1, levels, 1, R, S), BF16),
-            jax.ShapeDtypeStruct((rows, R, S), BF16),
+            pltpu.VMEM((1, levels, 1, R, S), BF16),
+            pltpu.VMEM((rows, R, S), BF16),
         ),
         in_specs=[pl.BlockSpec(memory_space=pl.ANY)] * len(operands),
         out_specs=(pl.BlockSpec(memory_space=pltpu.VMEM),) * 2,

time: 77 us -> 74.3 us (0.965)
  Pallas kernels: 74.1 us -> 71.5 us
  local copies, waits for them, and re-layouts: 2.09 us -> 1.25 us
    pallas_call x1, Pallas kernels: 74.1 us -> 71.5 us  [per_device(): pl.pallas_call(functools.partial(kernel, nl, ny, nz, levels, rows, rq, S)...]
    unnamed x4 -> x2, local copies, waits for them, and re-layouts: 2.09 us -> 1.25 us
where the time goes in v4:
time: 74.3 us; the launch traced here: 73.4 us
  Pallas kernels  71.5 us (96%)
  local copies, waits for them, and re-layouts  1.25 us (2%)
    pallas_call x1, Pallas kernels, per_device(): pl.pallas_call(functools.partial(kernel, nl, ny, nz, levels, rows, rq, S)...  71.5 us

profile of v4, /device:TPU:6, one launch (start us, length us, event | category | flops | bytes accessed | tf_op | source)
XLA Modules:
  0.0 73.4 jit_solution(14809063454897848878)
XLA Ops:
  0.6 71.5 %solve.1 = (bf16[1,3,1,64,128]{4,3,2,1,0:T(8,128)(2,1)S(1)}, bf16[4,64,128]{2,1,0:T(8,128)(2,1)S(1)}) custom-call(bf16[1,3,4,64,128]{4,3,2,1,0:T(8,128)(2,1)} %rhs.1, bf16[1,3,4,128,128]{4,3,2,1,0:T(8,128)(2,1)} %diag_low.1, bf16[1,3,1,128,128]{4,3,2,1,0:T(8,128)(2,1)} %diag_up.1, bf16[1,2,4,1,128,128]{5,4,3,2,1,0:T(8,128)(2,1)} %low.1, ...), custom_call_target="tpu_custom_call" | custom-call | tf_op jit(solution)/shard_map/solve/pallas_call | solution.py:483
  72.2 0.6 copy.18
  72.8 0.6 copy.19
